TPU v7x, 32 devices: a whole 2x2x4 slice. The times are simulated.
32 devices in a mesh: groups: 2 (over x), row: 16 (over z, y, core).
Axes of the slice: x: 2, y: 2, z: 4, core: 2. Of those that a mesh axis runs over, the one named last changes fastest.
Arguments:
- panels: bfloat16 [512, 8, 256], P(('groups', 'row')), parts along dimension 0, may hold values from -6 to 6
- diag_blocks: bfloat16 [512, 256, 256], P(('groups', 'row')), parts along dimension 0, may hold values from -0.1875 to 0.1875
- near_blocks: bfloat16 [512, 2, 256, 256], P(('groups', 'row')), parts along dimension 0, may hold values from -0.1875 to 0.1875
- near_offsets: int32 [512, 2], P(('groups', 'row')), parts along dimension 0, may hold values from 1 to 4
- far_u: bfloat16 [6144, 32, 256], P(('groups', 'row')), parts along dimension 0, may hold values from -0.375 to 0.375
- far_v: bfloat16 [6144, 32, 256], P(('groups', 'row')), parts along dimension 0, may hold values from -0.375 to 0.375
- far_row: int32 [6144], P(('groups', 'row')), parts along dimension 0, may hold values from 0 to 15
- far_owner: int32 [6144, 1], P(('groups', 'row')), parts along dimension 0, may hold values from 0 to 15; in each aligned block of 192 rows (0 to 191, 192 to 383, ...) at most 24 rows name the same one
- far_slot: int32 [6144], P(('groups', 'row')), parts along dimension 0, may hold values from 0 to 15
Outputs:
- product: float32 [512, 8, 256], P(('groups', 'row')), parts along dimension 0
There are 2 independent parts, one for each index of `groups`. A program takes and returns all parts, laid end to end along the dimension named above; each array names one. Nothing has to cross between parts.
Inputs may be any that keep to these rules, and one draw needn't show every extreme that they name: `far_owner`: within the 192 rows of one device (aligned blocks of rows), no owner is named more than 24 times, a bound that some block reaches.
All inputs are finite; a program needn't handle non-finite values.
Results may differ from a plain program's by a relative error of at most 0.0025.
Values may be sent and summed in bfloat16 or wider, within the bound.
A program may use at most 128 MiB of HBM per device.

v0:
```python
import jax
import jax.numpy as jnp
from jax import lax
from jax.sharding import PartitionSpec as P

REACH = 4


def from_behind(value, axis, steps):
    count = lax.axis_size(axis)
    first, last = (max(0, -steps), min(count, count - steps))
    return lax.ppermute(value, axis, [(source, source + steps) for source in range(first, last)])


def local(
    panels, diag_blocks, near_blocks, near_offsets, far_u, far_v, far_row, far_owner, far_slot
):
    leaf_count, rhs_count, leaf_width = panels.shape
    columns = rhs_count * leaf_width
    near_count = near_blocks.shape[1]
    peer_count = lax.axis_size("row")
    far_count = far_row.shape[0]
    capacity = 2 * far_count // peer_count
    slot_count = peer_count * capacity
    highest = lax.Precision.HIGHEST
    result = jnp.einsum(
        "inl,ilm->inm", panels, diag_blocks, preferred_element_type=jnp.float32
    ).reshape(leaf_count, columns)
    following = from_behind(panels[:REACH], "row", -1)
    extended = jnp.concatenate([panels, following], axis=0).reshape(leaf_count + REACH, columns)
    target = jnp.arange(leaf_count, dtype=jnp.int32)[:, None] + near_offsets
    picking = (
        target.reshape(-1)[:, None] == jnp.arange(leaf_count + REACH, dtype=jnp.int32)[None, :]
    )
    near_x = jnp.dot(
        picking.astype(jnp.bfloat16), extended, preferred_element_type=jnp.float32
    ).astype(jnp.bfloat16)
    near_x = near_x.reshape(leaf_count, near_count, rhs_count, leaf_width)
    near_forward = jnp.einsum(
        "iknl,ikml->inm", near_x, near_blocks, preferred_element_type=jnp.float32
    )
    result = result + near_forward.reshape(leaf_count, columns)
    backward = jnp.einsum("inl,iklm->iknm", panels, near_blocks, preferred_element_type=jnp.float32)
    spread = jnp.einsum(
        "re,rc->ec",
        picking.astype(jnp.float32),
        backward.reshape(leaf_count * near_count, columns),
        precision=highest,
    )
    result = result + spread[:leaf_count]
    incoming = from_behind(spread[leaf_count:].astype(jnp.bfloat16), "row", 1).astype(jnp.float32)
    result = result.at[:REACH].add(incoming)
    owners = far_owner[:, 0]
    owner_hits = (owners[:, None] == jnp.arange(peer_count, dtype=jnp.int32)[None, :]).astype(
        jnp.int32
    )
    position = jnp.sum((jnp.cumsum(owner_hits, axis=0) - owner_hits) * owner_hits, axis=1)
    slot_of = owners * capacity + position
    placing = slot_of[:, None] == jnp.arange(slot_count, dtype=jnp.int32)[None, :]
    row_panels = jnp.take(panels, far_row, axis=0)
    projected = jnp.einsum(
        "pnl,prl->pnr", row_panels, far_u, preferred_element_type=jnp.float32
    ).astype(jnp.bfloat16)
    returned = jnp.einsum("pnr,prl->pnl", projected, far_v, preferred_element_type=jnp.float32)
    send_ids = jnp.sum(jnp.where(placing, far_slot[:, None], 0), axis=0)
    send_terms = jnp.einsum(
        "ps,pc->sc",
        placing.astype(jnp.float32),
        returned.reshape(far_count, columns),
        precision=highest,
    )
    got_ids, got_terms = (
        lax.all_to_all(send_ids, "row", split_axis=0, concat_axis=0, tiled=True),
        lax.all_to_all(send_terms, "row", split_axis=0, concat_axis=0, tiled=True),
    )
    landing = got_ids[:, None] == jnp.arange(leaf_count, dtype=jnp.int32)[None, :]
    result = result + jnp.einsum(
        "sl,sc->lc", landing.astype(jnp.float32), got_terms, precision=highest
    )
    everything = lax.all_gather(panels, "row", axis=0, tiled=True)
    col_panels = jnp.take(everything, owners * leaf_count + far_slot, axis=0)
    reduced = jnp.einsum(
        "pnl,prl->pnr", col_panels, far_v, preferred_element_type=jnp.float32
    ).astype(jnp.bfloat16)
    forward = jnp.einsum("pnr,prl->pnl", reduced, far_u, preferred_element_type=jnp.float32)
    row_hits = (far_row[:, None] == jnp.arange(leaf_count, dtype=jnp.int32)[None, :]).astype(
        jnp.float32
    )
    result = result + jnp.einsum(
        "pi,pc->ic", row_hits, forward.reshape(far_count, columns), precision=highest
    )
    return result.reshape(leaf_count, rhs_count, leaf_width)


def solution(mesh):
    return jax.shard_map(
        local,
        mesh=mesh,
        in_specs=(
            P(("groups", "row"), None, None),
            P(("groups", "row"), None, None),
            P(("groups", "row"), None, None, None),
            P(("groups", "row"), None),
            P(("groups", "row"), None, None),
            P(("groups", "row"), None, None),
            P(("groups", "row")),
            P(("groups", "row"), None),
            P(("groups", "row")),
        ),
        out_specs=P(("groups", "row"), None, None),
        check_vma=False,
    )
```

profile of v0, /device:TPU:15, one launch (start us, length us, event | category | flops | bytes accessed | tf_op | source)
XLA Modules:
  0.0 140.9 jit_solution(12363072589930008576)
XLA Ops:
  6.5 0.0 copy-start
  6.5 0.8 iota_compare_fusion.5
  7.4 0.6 reduce-window.6
  8.0 0.2 slice_reduce_fusion
  8.2 0.1 bitcast_bitcast_fusion
  8.3 0.7 fusion.27
  9.0 0.7 multiply_add_fusion.1
  9.7 0.8 select_reduce_fusion
  10.5 0.7 all_to_all.12
  11.2 6.6 %all-to-all-start = ((s32[16,24,1]{1,2,0:T(1,128)}), s32[16,24,1]{1,2,0:T(1,128)S(1)}, u32[]{:S(2)}, u32[]{:S(2)}) async-start(s32[16,24,1]{1,2,0:T(1,128)} %bitcast.9), calls=%async_computation | async-start | bytes 16384 | tf_op jit(solution)/shard_map/all_to_all | solution.py:73
  17.7 0.7 compare_select_fusion.1
  18.4 0.7 compare_and_fusion.1
  19.1 2.5 %gather_fusion = bf16[192,8,256]{2,1,0:T(8,128)(2,1)} fusion(bf16[16,8,256]{2,1,0:T(8,128)(2,1)} %param.11, s32[1024]{0:T(1024)S(1)} %pad_clamp_fusion.1), kind=kCustom, calls=%fused_computation | custom fusion | bytes 1573632 | tf_op jit(solution)/shard_map/jit(_take)/gather | solution.py:60
  21.7 0.0 copy-done
  21.7 4.7 %fusion.1 = f32[192,8,256]{2,1,0:T(8,128)} fusion(bf16[192,32,256]{2,1,0:T(8,128)(2,1)} %param.16, bf16[192,32,256]{2,1,0:T(8,128)(2,1)S(1)} %copy-done, bf16[192,8,256]{2,1,0:T(8,128)(2,1)} %gather_fusion, pred[192]{0:T(512)(128)(4,1)S(1)} %compare_and_fusion.1), kind=kOutput, calls=%fused_computation.7 | convolution fusion | flops 50774016 | bytes 8650944 | tf_op jit(solution)/shard_map/pnr,prl->pnl/dot_general | solution.py:64
  26.4 2.5 %reshape.125 = f32[192,2048,1]{1,0,2:T(8,128)} reshape(f32[192,8,256]{2,1,0:T(8,128)} %fusion.1) | data formatting | bytes 3145728 | tf_op jit(solution)/shard_map/reshape | solution.py:69
  28.9 4.6 %fusion.16 = f32[16,24,2048]{2,1,0:T(8,128)} fusion(f32[192,2048,1]{1,0,2:T(8,128)} %reshape.125, s32[16,24]{1,0:T(8,128)S(1)} %multiply_add_fusion, s32[192]{0:T(256)S(1)} %bitcast.73), kind=kOutput, calls=%fused_computation.17 | convolution fusion | flops 1812013056 | bytes 4720896 | tf_op jit(solution)/shard_map/ps,pc->sc/dot_general | solution.py:66
  33.4 0.0 copy-start.1
  33.4 0.0 copy-start.6
  33.5 0.0 all-to-all-done
  33.5 6.2 %all-to-all-start.1 = ((f32[16,24,2048]{2,1,0:T(8,128)}), f32[16,24,2048]{2,1,0:T(8,128)}, u32[]{:S(2)}, u32[]{:S(2)}) async-start(f32[16,24,2048]{2,1,0:T(8,128)} %fusion.16), calls=%async_computation.1 | async-start | bytes 6291456 | tf_op jit(solution)/shard_map/all_to_all | solution.py:74
  39.6 0.0 copy-start.3
  39.6 0.0 copy-start.5
  39.6 0.0 all-gather.2.cloned.1.call-start
  39.7 0.7 all-gather.2.cloned.1.call-update
  40.4 0.0 copy-done.1
  40.4 2.3 %collective-permute-start = (bf16[4,8,256]{2,1,0:T(8,128)(2,1)S(1)}, bf16[4,8,256]{2,1,0:T(8,128)(2,1)S(1)}, u32[]{:S(2)}, u32[]{:S(2)}) collective-permute-start(bf16[4,8,256]{2,1,0:T(8,128)(2,1)S(1)} %slice.38), channel_id=1, source_target_pairs={{1,0},{2,1},{3,2},{4,3},{5,4},{6,5},{7,6},{8,7},{9,8},{10,9},{11,1... | collective-permute-start | bytes 49160 | tf_op jit(solution)/shard_map/ppermute | solution.py:12
  42.7 0.0 copy-done.6
  42.7 0.1 copy.18
  42.8 0.1 eq.102
  42.9 0.0 copy-start.2
  42.9 3.0 %fusion.22 = f32[16,2,256,8]{2,3,1,0:T(8,128)S(1)} fusion(bf16[16,2,256,256]{3,2,1,0:T(8,128)(2,1)} %param.13, bf16[16,8,256]{2,1,0:T(8,128)(2,1)S(1)} %copy-done.1), kind=kOutput, calls=%fused_computation.29 | convolution fusion | flops 33554432 | bytes 4521984 | tf_op jit(solution)/shard_map/inl,iklm->iknm/dot_general | solution.py:43
  45.9 0.1 copy.29
  46.0 0.4 fusion.28
  46.3 4.2 %collective-permute-start.1 = (bf16[4,2048]{1,0:T(4,128)(2,1)S(1)}, bf16[4,2048]{1,0:T(4,128)(2,1)S(1)}, u32[]{:S(2)}, u32[]{:S(2)}) collective-permute-start(bf16[4,2048]{1,0:T(4,128)(2,1)S(1)} %slice.65), channel_id=1, source_target_pairs={{0,1},{1,2},{2,3},{3,4},{4,5},{5,6},{6,7},{7,8},{8,9},{9,10},{10,1... | collective-permute-start | bytes 49160 | tf_op jit(solution)/shard_map/ppermute | solution.py:12
  50.5 0.0 copy-done.3
  50.5 0.0 copy-done.5
  50.6 0.0 copy-done.2
  50.6 1.0 fusion.35
  51.6 0.6 broadcast.71
  52.2 0.7 reduce.7
  52.9 0.1 eq.117
  53.0 63.0 %collective-permute-done = bf16[4,8,256]{2,1,0:T(8,128)(2,1)S(1)} collective-permute-done((bf16[4,8,256]{2,1,0:T(8,128)(2,1)S(1)}, bf16[4,8,256]{2,1,0:T(8,128)(2,1)S(1)}, u32[]{:S(2)}, u32[]{:S(2)}) %collective-permute-start) | collective-permute-done | bytes 16416 | tf_op jit(solution)/shard_map/ppermute | solution.py:12
  116.1 0.2 convolution_convert_fusion
  116.4 3.4 %fusion.3 = f32[16,8,256]{2,1,0:T(8,128)S(1)} fusion(f32[16,8,256]{2,1,0:T(8,128)} %fusion.35, bf16[16,2,8,256]{3,2,1,0:T(8,128)(2,1)S(1)} %bitcast.63, bf16[16,2,256,256]{3,2,1,0:T(8,128)(2,1)} %param.13), kind=kOutput, calls=%fused_computation.10 | convolution fusion | flops 33587200 | bytes 4587520 | tf_op jit(solution)/shard_map/iknl,ikml->inm/dot_general | solution.py:39
  119.7 0.1 copy.28
  119.8 0.0 collective-permute-done.1
  119.9 0.0 all-gather.2.cloned.1.call-done
  119.9 3.0 %gather_fusion.1 = bf16[192,8,256]{2,1,0:T(8,128)(2,1)} fusion(bf16[256,8,256]{2,1,0:T(8,128)(2,1)} %all-gather.2.cloned.1.call-done, s32[1024]{0:T(1024)S(1)} %pad_clamp_fusion), kind=kCustom, calls=%fused_computation.1 | custom fusion | bytes 1573632 | tf_op jit(solution)/shard_map/jit(_take)/gather | solution.py:81
  122.9 4.7 %fusion.2 = f32[192,8,256]{2,1,0:T(8,128)} fusion(bf16[192,32,256]{2,1,0:T(8,128)(2,1)S(1)} %copy-done, bf16[192,32,256]{2,1,0:T(8,128)(2,1)} %param.16, bf16[192,8,256]{2,1,0:T(8,128)(2,1)} %gather_fusion.1, pred[192]{0:T(512)(128)(4,1)S(1)} %get-tuple-element.17), kind=kOutput, calls=%fused_computation.8 | convolution fusion | flops 50774016 | bytes 8650944 | tf_op jit(solution)/shard_map/pnr,prl->pnl/dot_general | solution.py:85
  127.6 0.0 copy-start.4
  127.6 2.0 %copy.30 = f32[24,8,8,256]{3,1,2,0:T(8,128)S(1)} copy(f32[24,8,8,256]{3,2,1,0:T(8,128)} %bitcast.59) | data formatting | bytes 3145728
  129.6 0.0 copy-done.4
  129.6 0.7 fusion.21
  130.3 0.0 all-to-all-done.1
  130.3 3.1 %fusion = f32[16,2048]{1,0:T(8,128)S(1)} fusion(f32[16,2048]{1,0:T(8,128)S(1)} %fusion.21, f32[16,2048]{1,0:T(8,128)S(1)} %fusion.25, f32[384,2048]{1,0:T(8,128)} %bitcast.10, s32[384]{0:T(512)S(1)} %eq.117), kind=kOutput, calls=%fused_computation.4 | convolution fusion | flops 151066624 | bytes 3540480 | tf_op jit(solution)/shard_map/sl,sc->lc/dot_general | solution.py:77
  133.3 0.7 copy.31
  (16 shorter events, 0.2 us)
Async XLA Ops:
  6.5 15.1 %copy-start = (bf16[192,32,256]{2,1,0:T(8,128)(2,1)S(1)}, bf16[192,32,256]{2,1,0:T(8,128)(2,1)}, u32[]{:S(2)}) copy-start(bf16[192,32,256]{2,1,0:T(8,128)(2,1)} %param.15) | copy-start | bytes 9437188
  11.2 22.3 %all-to-all-start = ((s32[16,24,1]{1,2,0:T(1,128)}), s32[16,24,1]{1,2,0:T(1,128)S(1)}, u32[]{:S(2)}, u32[]{:S(2)}) async-start(s32[16,24,1]{1,2,0:T(1,128)} %bitcast.9), calls=%async_computation | async-start | bytes 16384 | tf_op jit(solution)/shard_map/all_to_all | solution.py:73
  33.4 6.9 %copy-start.1 = (bf16[16,8,256]{2,1,0:T(8,128)(2,1)S(1)}, bf16[16,8,256]{2,1,0:T(8,128)(2,1)}, u32[]{:S(2)}) copy-start(bf16[16,8,256]{2,1,0:T(8,128)(2,1)} %param.11) | copy-start | bytes 196612
  33.4 9.2 %copy-start.6 = (s32[16,2]{0,1:T(2,128)S(1)}, s32[16,2]{0,1:T(2,128)}, u32[]{:S(2)}) copy-start(s32[16,2]{0,1:T(2,128)} %param.14) | copy-start | bytes 388
  33.5 96.8 %all-to-all-start.1 = ((f32[16,24,2048]{2,1,0:T(8,128)}), f32[16,24,2048]{2,1,0:T(8,128)}, u32[]{:S(2)}, u32[]{:S(2)}) async-start(f32[16,24,2048]{2,1,0:T(8,128)} %fusion.16), calls=%async_computation.1 | async-start | bytes 6291456 | tf_op jit(solution)/shard_map/all_to_all | solution.py:74
  39.6 10.9 %copy-start.3 = (s32[192,1]{0,1:T(1,128)S(1)}, s32[192,1]{0,1:T(1,128)}, u32[]{:S(2)}) copy-start(s32[192,1]{0,1:T(1,128)} %param.18) | copy-start | bytes 2308
  39.6 10.9 %copy-start.5 = (s32[192]{0:T(256)S(1)}, s32[192]{0:T(256)}, u32[]{:S(2)}) copy-start(s32[192]{0:T(256)} %param.19) | copy-start | bytes 2308
  39.6 80.2 %all-gather.2.cloned.1.call-start = ((), (), s32[]{:S(2)}) async-start(), calls=%async_computation.2 | async-start | bytes 1114112 | tf_op jit(solution)/shard_map/all_gather | solution.py:80
  40.4 75.7 %collective-permute-start = (bf16[4,8,256]{2,1,0:T(8,128)(2,1)S(1)}, bf16[4,8,256]{2,1,0:T(8,128)(2,1)S(1)}, u32[]{:S(2)}, u32[]{:S(2)}) collective-permute-start(bf16[4,8,256]{2,1,0:T(8,128)(2,1)S(1)} %slice.38), channel_id=1, source_target_pairs={{1,0},{2,1},{3,2},{4,3},{5,4},{6,5},{7,6},{8,7},{9,8},{10,9},{11,1... | collective-permute-start | bytes 49160 | tf_op jit(solution)/shard_map/ppermute | solution.py:12
  42.9 7.7 %copy-start.2 = (bf16[16,256,256]{2,1,0:T(8,128)(2,1)S(1)}, bf16[16,256,256]{2,1,0:T(8,128)(2,1)}, u32[]{:S(2)}) copy-start(bf16[16,256,256]{2,1,0:T(8,128)(2,1)} %param.12) | copy-start | bytes 6291460
  46.3 73.5 %collective-permute-start.1 = (bf16[4,2048]{1,0:T(4,128)(2,1)S(1)}, bf16[4,2048]{1,0:T(4,128)(2,1)S(1)}, u32[]{:S(2)}, u32[]{:S(2)}) collective-permute-start(bf16[4,2048]{1,0:T(4,128)(2,1)S(1)} %slice.65), channel_id=1, source_target_pairs={{0,1},{1,2},{2,3},{3,4},{4,5},{5,6},{6,7},{7,8},{8,9},{9,10},{10,1... | collective-permute-start | bytes 49160 | tf_op jit(solution)/shard_map/ppermute | solution.py:12
  127.6 2.0 %copy-start.4 = (s32[192]{0:T(256)S(1)}, s32[192]{0:T(256)}, u32[]{:S(2)}) copy-start(s32[192]{0:T(256)} %param.17) | copy-start | bytes 2308
Sparse Core Ops, SparseCore 0:
  42.6 64.0 all-gather.1
where the time goes:
time: 141 us
  waiting for transfers between devices  63.7 us (45%)
  matrix products  25.6 us (18%)
  starting transfers between devices  19.2 us (14%)
  between operations  13.6 us (10%)
  local copies, waits for them, and re-layouts  12.8 us (9%)
  other arithmetic  5.9 us (4%)
    ppermute x2, waiting for transfers between devices, from_behind(): lax.ppermute(value, axis, [(source, source + steps) for source in range(f...  63 us
    all_to_all x1, starting transfers between devices, local(): lax.all_to_all(send_ids, 'row', split_axis=0, concat_axis=0, tiled=True)  6.55 us
    ppermute x2, starting transfers between devices, from_behind(): lax.ppermute(value, axis, [(source, source + steps) for source in range(f...  6.46 us
    all_to_all x1, starting transfers between devices, local(): lax.all_to_all(send_terms, 'row', split_axis=0, concat_axis=0, tiled=True)  6.16 us
    dot_general x1, matrix products, local(): jnp.einsum('pnr,prl->pnl', projected, far_v, preferred_element_type=jnp.f...  4.69 us
    dot_general x1, matrix products, local(): jnp.einsum('pnr,prl->pnl', reduced, far_u, preferred_element_type=jnp.flo...  4.68 us
    dot_general x1, matrix products, local(): jnp.einsum('ps,pc->sc', placing.astype(jnp.float32), returned.reshape(far...  4.57 us
    dot_general x1, matrix products, local(): jnp.einsum('iknl,ikml->inm', near_x, near_blocks, preferred_element_type=...  3.37 us
  transfers between devices with their start and end apart: 5, of which 1 were waited for; matrix products, arithmetic and copies ran while one was open for 25% of the time, Pallas kernels for 0%

commit v1 on v0

v1 whole, which is shorter than its diff:
```python
import functools

import jax
import jax.numpy as jnp
from jax import lax
from jax.experimental import pallas as pl
from jax.experimental.pallas import tpu as pltpu
from jax.sharding import PartitionSpec as P

REACH = 4
GROUP = 16
F32, BF16 = jnp.float32, jnp.bfloat16


def dot(a, b):
    return lax.dot_general(a, b, (((1,), (0,)), ((), ())), preferred_element_type=F32)


def dot_t(a, b):
    return lax.dot_general(a, b, (((1,), (1,)), ((), ())), preferred_element_type=F32)


def eye(count):
    return lax.broadcasted_iota(jnp.int32, (count, count), 0) == lax.broadcasted_iota(
        jnp.int32, (count, count), 1
    )


def to_column(row):
    return jnp.sum(jnp.where(eye(row.shape[1]), row, 0), axis=1, keepdims=True)


def to_row(column):
    return jnp.sum(jnp.where(eye(column.shape[0]), column, 0), axis=0, keepdims=True)


def hits_wide(column, count):
    shape = (column.shape[0], count)
    return (column == lax.broadcasted_iota(jnp.int32, shape, 1)).astype(F32).astype(BF16)


def hits_tall(row, count):
    shape = (count, row.shape[1])
    return (row == lax.broadcasted_iota(jnp.int32, shape, 0)).astype(F32).astype(BF16)


def split(value):
    high = value.astype(BF16)
    return high, (value - high.astype(F32)).astype(BF16)


def scatter_rows(places, value):
    high, low = split(value)
    return dot(places, high) + dot(places, low)


def far_pass(picked, first, second, terms):
    rhs, pairs, width = picked.shape
    rank = first.shape[1]
    rows, lanes = rhs * GROUP, GROUP * rank
    row_pair = lax.broadcasted_iota(jnp.int32, (rows, lanes), 0) % GROUP
    lane_pair = lax.broadcasted_iota(jnp.int32, (rows, lanes), 1) // rank
    block = (row_pair == lane_pair).astype(F32).astype(BF16)

    def step(t, carry):
        here = pl.ds(pl.multiple_of(t * GROUP, GROUP), GROUP)
        left = picked[:, here, :].reshape(rows, width)
        one = first[here].reshape(lanes, width)
        two = second[here].reshape(lanes, width)
        inner = dot_t(left, one).astype(BF16) * block
        terms[:, here, :] = dot(inner, two).reshape(rhs, GROUP, width)
        return carry

    lax.fori_loop(0, pairs // GROUP, step, 0, unroll=2)


def near_terms(i, leaf_x, near_x, diag, near, off, acc):
    x = leaf_x.astype(BF16)
    acc[i] += dot(x, diag[i])
    for k in range(near.shape[1]):
        acc[i] += dot_t(near_x(i + off[i, k]).astype(BF16), near[i, k])
        back = dot(x, near[i, k])
        for d in range(1, REACH + 1):
            acc[i + d] += jnp.where(off[i, k] == d, back, 0.0)


def kernel(
    panels, diag_h, near_h, off, u_h, v_h, far_row, far_owner, far_slot, everything,
    out, sums,
    u, v, diag, near, x32, acc, picked, terms, sems,
):
    loads = [
        pltpu.make_async_copy(a, b, sems.at[s])
        for s, (a, b) in enumerate(((u_h, u), (v_h, v), (near_h, near), (diag_h, diag)))
    ]
    for load in loads:
        load.start()
    leaves, rhs, width = panels.shape
    peers = everything.shape[0]
    me = lax.axis_index("row")
    final = me == peers - 1
    following = jnp.minimum(me + 1, peers - 1)
    acc[...] = jnp.zeros_like(acc)
    x32[:leaves] = panels[...].astype(F32)
    for n in range(rhs):
        ahead = everything[following, n].astype(F32)[:REACH]
        x32[leaves:, n, :] = jnp.where(final, 0.0, ahead)

    rows_wide = hits_wide(to_column(far_row[...]), leaves)
    for n in range(rhs):
        picked[n] = dot(rows_wide, x32[:leaves, n, :].astype(BF16)).astype(BF16)
    loads[0].wait()
    loads[1].wait()
    far_pass(picked, u, v, terms)
    ids = to_row(far_owner[...]) * leaves + far_slot[...]
    places = hits_tall(ids, peers * leaves)
    for n in range(rhs):
        sums[:, n] = scatter_rows(places, terms[n]).astype(BF16).reshape(peers, leaves, width)

    loads[2].wait()
    loads[3].wait()

    def step(i, carry):
        near_terms(i, x32[i], lambda j: x32[j], diag, near, off, acc)
        return carry

    lax.fori_loop(0, leaves, step, 0, unroll=2)
    for n in range(rhs):
        spill = jnp.where(final, 0.0, acc[leaves:, n, :])
        spill = jnp.concatenate([spill, jnp.zeros((leaves - REACH, width), F32)], axis=0)
        sums[following, n] = (sums[following, n].astype(F32) + spill).astype(BF16)

    ids_wide = hits_wide(far_owner[...] * leaves + to_column(far_slot[...]), peers * leaves)
    for n in range(rhs):
        table = everything[:, n].reshape(peers * leaves, width)
        picked[n] = dot(ids_wide, table).astype(BF16)
    far_pass(picked, v, u, terms)
    rows_tall = hits_tall(far_row[...], leaves)
    for n in range(rhs):
        out[:, n, :] = acc[:leaves, n, :] + scatter_rows(rows_tall, terms[n])


def local(panels, diag_blocks, near_blocks, near_offsets, far_u, far_v, far_row, far_owner, far_slot):
    leaves, rhs, width = panels.shape
    pairs = far_row.shape[0]
    peers = lax.axis_size("row")
    everything = lax.all_gather(jnp.swapaxes(panels, 0, 1), "row", axis=0)
    vmem, anywhere = (pl.BlockSpec(memory_space=m) for m in (pltpu.VMEM, pl.ANY))
    out, sums = pl.pallas_call(
        kernel,
        out_shape=(
            jax.ShapeDtypeStruct(panels.shape, F32),
            jax.ShapeDtypeStruct((peers, rhs, leaves, width), BF16),
        ),
        in_specs=[
            vmem, anywhere, anywhere, pl.BlockSpec(memory_space=pltpu.SMEM),
            anywhere, anywhere, vmem, vmem, vmem, vmem,
        ],
        out_specs=(vmem, vmem),
        scratch_shapes=[
            pltpu.VMEM(far_u.shape, BF16),
            pltpu.VMEM(far_v.shape, BF16),
            pltpu.VMEM(diag_blocks.shape, BF16),
            pltpu.VMEM(near_blocks.shape, BF16),
            pltpu.VMEM((leaves + REACH, rhs, width), F32),
            pltpu.VMEM((leaves + REACH, rhs, width), F32),
            pltpu.VMEM((rhs, pairs, width), BF16),
            pltpu.VMEM((rhs, pairs, width), F32),
            pltpu.SemaphoreType.DMA((4,)),
        ],
        compiler_params=pltpu.CompilerParams(vmem_limit_bytes=56 << 20),
    )(
        panels, diag_blocks, near_blocks, near_offsets, far_u, far_v,
        far_row.reshape(1, pairs), far_owner, far_slot.reshape(1, pairs), everything,
    )
    got = lax.all_to_all(sums, "row", split_axis=0, concat_axis=0, tiled=True)
    return out + jnp.swapaxes(jnp.sum(got.astype(F32), axis=0), 0, 1)


def solution(mesh):
    split_all = ("groups", "row")
    return jax.shard_map(
        local,
        mesh=mesh,
        in_specs=tuple(P(split_all) for _ in range(9)),
        out_specs=P(split_all),
        check_vma=False,
    )
```

time: 141 us -> 106 us (0.75)
  the two profiles are of different devices: /device:TPU:15 before, /device:TPU:0 now
where the time goes in v1:
time: 106 us; the launch traced here: 105 us
  waiting for transfers between devices  39.7 us (37%)
  blocking collectives  29.2 us (28%)
  Pallas kernels  16.5 us (16%)
  between operations  13.4 us (13%)
  local copies, waits for them, and re-layouts  5.59 us (5%)
    all_gather x1, waiting for transfers between devices, local(): everything = lax.all_gather(jnp.swapaxes(panels, 0, 1), 'row', axis=0)  39 us
    all_to_all x1, blocking collectives, local(): got = lax.all_to_all(sums, 'row', split_axis=0, concat_axis=0, tiled=True)  29.2 us
    pallas_call x1, Pallas kernels, local(): pl.pallas_call(kernel, out_shape=(jax.ShapeDtypeStruct(panels.shape, F32)...  16.5 us
    unnamed x4, local copies, waits for them, and re-layouts  2.81 us
    all_gather x1, local copies, waits for them, and re-layouts, local(): everything = lax.all_gather(jnp.swapaxes(panels, 0, 1), 'row', axis=0)  2.78 us
  transfers between devices with their start and end apart: 1, of which 1 were waited for; matrix products, arithmetic and copies ran while one was open for 3% of the time, Pallas kernels for 0%

profile of v1, /device:TPU:0, one launch (start us, length us, event | category | flops | bytes accessed | tf_op | source)
XLA Modules:
  0.0 105.2 jit_solution(9827990096493065730)
XLA Ops:
  6.5 0.0 all-gather.3.cloned.1.call-start
  6.5 0.7 all-gather.3.cloned.1.call-update
  7.3 1.4 %copy.14.off = s32[16,2]{1,0:T(8,128)} copy(s32[16,2]{0,1:T(2,128)} %param.12) | data formatting | bytes 256 | tf_op args[3]
  8.6 1.4 %copy.15.far_owner = s32[192,1]{1,0:T(8,128)} copy(s32[192,1]{0,1:T(1,128)} %param.16) | data formatting | bytes 1536 | tf_op args[7]
  10.1 39.0 %all-gather.3.cloned.1.call-done = bf16[128,16,256]{2,0,1:T(8,128)(2,1)} async-done(((bf16[8,16,256]{2,0,1:T(8,128)(2,1)}), bf16[128,16,256]{2,0,1:T(8,128)(2,1)}) %all-gather.3.cloned.1.call-update) | async-done | bytes 1048592 | tf_op jit(solution)/shard_map/all_gather | solution.py:147
  49.1 2.8 %copy.13 = bf16[128,16,256]{2,1,0:T(8,128)(2,1)} copy(bf16[128,16,256]{2,0,1:T(8,128)(2,1)} %all-gather.3.cloned.1.call-done) | data formatting | bytes 2097152 | tf_op jit(solution)/shard_map/all_gather | solution.py:147
  51.8 16.5 %shard_map.91 = (f32[16,8,256]{2,1,0:T(8,128)}, bf16[16,8,16,256]{3,2,1,0:T(8,128)(2,1)}) custom-call(bf16[16,8,256]{2,1,0:T(8,128)(2,1)} %panels.1, bf16[16,256,256]{2,1,0:T(8,128)(2,1)} %diag_h.1, bf16[16,2,256,256]{3,2,1,0:T(8,128)(2,1)} %near_h.1, s32[16,2]{1,0:T(8,128)} %copy.14.off, bf16[192,32,256]{2,1,0:T(8,128)(2,1)} %u_h.1, ...), custom_call_target="tpu_custom_call" | custom-call | tf_op jit(solution)/shard_map/pallas_call | solution.py:149
  68.3 0.0 copy-start
  68.3 29.2 %all_to_all.5 = bf16[16,8,16,256]{3,2,1,0:T(8,128)(2,1)S(1)} all-to-all(bf16[16,8,16,256]{3,2,1,0:T(8,128)(2,1)} %get-tuple-element.8), channel_id=1, replica_groups=mesh['groups'=2,'row'=16] {'row'}, dimensions={0} | all-to-all | bytes 2097152 | tf_op jit(solution)/shard_map/all_to_all | solution.py:176
  97.5 0.1 convert_reduce_fusion
  97.6 0.0 copy-done
  97.7 0.7 bitcast_add_fusion
Async XLA Ops:
  6.5 42.5 %all-gather.3.cloned.1.call-start = ((), (), s32[]{:S(2)}) async-start(), calls=%async_computation.1 | async-start | bytes 1114112 | tf_op jit(solution)/shard_map/all_gather | solution.py:147
  68.3 29.3 %copy-start = (f32[16,8,256]{2,1,0:T(8,128)S(1)}, f32[16,8,256]{2,1,0:T(8,128)}, u32[]{:S(2)}) copy-start(f32[16,8,256]{2,1,0:T(8,128)} %get-tuple-element.7) | copy-start | bytes 393220
Sparse Core Ops, SparseCore 0:
  9.5 39.4 all-gather.2

commit v2 on v1

--- a/solution.py
+++ b/solution.py
@@ -54,7 +54,7 @@
     return dot(places, high) + dot(places, low)
 
 
-def far_pass(picked, first, second, terms):
+def far_pass(picked, first, second, terms, begin, end):
     rhs, pairs, width = picked.shape
     rank = first.shape[1]
     rows, lanes = rhs * GROUP, GROUP * rank
@@ -71,7 +71,7 @@
         terms[:, here, :] = dot(inner, two).reshape(rhs, GROUP, width)
         return carry
 
-    lax.fori_loop(0, pairs // GROUP, step, 0, unroll=2)
+    lax.fori_loop(begin, end, step, 0, unroll=2)
 
 
 def near_terms(i, leaf_x, near_x, diag, near, off, acc):
@@ -85,12 +85,16 @@
 
 
 def kernel(
-    panels, diag_h, near_h, off, u_h, v_h, far_row, far_owner, far_slot, everything,
-    out, sums,
-    u, v, diag, near, x32, acc, picked, terms, sems,
+    shape, panels, diag_h, near_h, off, u_h, v_h, far_row, far_owner, far_slot,
+    out,
+    u, v, diag, near, x32, acc, picked, terms, everything, sums,
+    got_core, pass_y, got_y, pass_z, got_z, spill, got_spill,
+    load_sem, send_z, recv_z, send_y, recv_y, send_c, recv_c,
+    send_1, recv_1, send_2, recv_2, send_3, recv_3, send_4, recv_4,
 ):
+    zs, ys = shape
     loads = [
-        pltpu.make_async_copy(a, b, sems.at[s])
+        pltpu.make_async_copy(a, b, load_sem.at[s])
         for s, (a, b) in enumerate(((u_h, u), (v_h, v), (near_h, near), (diag_h, diag)))
     ]
     for load in loads:
@@ -98,24 +102,100 @@
     leaves, rhs, width = panels.shape
     peers = everything.shape[0]
     me = lax.axis_index("row")
+    c = lax.rem(me, 2)
+    y = lax.rem(me // 2, ys)
+    z = me // (2 * ys)
     final = me == peers - 1
-    following = jnp.minimum(me + 1, peers - 1)
+    following = lax.rem(me + 1, peers)
+    preceding = lax.rem(me + peers - 1, peers)
+
+    def spot(zz, yy, cc):
+        return (zz * ys + yy) * 2 + cc
+
+    def up(d):
+        return lax.rem(z + d, zs)
+
+    def down(d):
+        return lax.rem(z + zs - d, zs)
+
+    sibling = spot(z, y, 1 - c)
+    beside = spot(z, 1 - y, c) if ys == 2 else None
+    column = [spot(up(d), y, c) for d in range(1, zs)]
+    greeted = [sibling] + ([beside] if ys == 2 else []) + column + [following, preceding]
+    barrier = pltpu.get_barrier_semaphore()
+    for peer in greeted:
+        pl.semaphore_signal(
+            barrier, inc=1, device_id={"row": peer}, device_id_type=pl.DeviceIdType.MESH
+        )
+
+    x32[:leaves] = panels[...].astype(F32)
+    x32[leaves:] = jnp.zeros((REACH, rhs, width), F32)
     acc[...] = jnp.zeros_like(acc)
-    x32[:leaves] = panels[...].astype(F32)
-    for n in range(rhs):
-        ahead = everything[following, n].astype(F32)[:REACH]
-        x32[leaves:, n, :] = jnp.where(final, 0.0, ahead)
+    for n in range(rhs):
+        everything[me, n] = x32[:leaves, n, :].astype(BF16)
+    pl.semaphore_wait(barrier, len(greeted))
+
+    sent = []
+
+    def send(source, target, send_sem, recv_sem, peer):
+        copy = pltpu.make_async_remote_copy(
+            src_ref=source, dst_ref=target, send_sem=send_sem, recv_sem=recv_sem,
+            device_id={"row": peer}, device_id_type=pl.DeviceIdType.MESH,
+        )
+        copy.start()
+        sent.append(copy)
+
+    def arrived(target, send_sem, recv_sem, peer):
+        pltpu.make_async_remote_copy(
+            src_ref=target, dst_ref=target, send_sem=send_sem, recv_sem=recv_sem,
+            device_id={"row": peer}, device_id_type=pl.DeviceIdType.MESH,
+        ).wait_recv()
+
+    def share(owner, peer, send_sem, recv_sem):
+        send(everything.at[owner], everything.at[owner], send_sem, recv_sem, peer)
+
+    def settled(owner, send_sem, recv_sem):
+        arrived(everything.at[owner], send_sem, recv_sem, sibling)
+
+    far_first = list(range(zs - 1, 0, -1))
+    for d in far_first:
+        share(me, column[d - 1], send_z.at[d], recv_z.at[d])
+    if ys == 2:
+        share(me, beside, send_y.at[0], recv_y.at[0])
+    share(me, sibling, send_c.at[0, 0], recv_c.at[0, 0])
 
     rows_wide = hits_wide(to_column(far_row[...]), leaves)
     for n in range(rhs):
         picked[n] = dot(rows_wide, x32[:leaves, n, :].astype(BF16)).astype(BF16)
     loads[0].wait()
     loads[1].wait()
-    far_pass(picked, u, v, terms)
+    groups = far_row.shape[1] // GROUP
+    far_pass(picked, u, v, terms, 0, groups // 2)
+    for d in range(1, zs):
+        owner = spot(down(d), y, c)
+        settled(owner, send_z.at[d], recv_z.at[d])
+        if ys == 2:
+            share(owner, beside, send_y.at[d], recv_y.at[d])
+        share(owner, sibling, send_c.at[0, d], recv_c.at[0, d])
+    far_pass(picked, u, v, terms, groups // 2, groups)
     ids = to_row(far_owner[...]) * leaves + far_slot[...]
     places = hits_tall(ids, peers * leaves)
     for n in range(rhs):
-        sums[:, n] = scatter_rows(places, terms[n]).astype(BF16).reshape(peers, leaves, width)
+        sums[:, :, n] = scatter_rows(places, terms[n]).astype(BF16).reshape(
+            peers // 2, 2, leaves, width
+        )
+
+    order = far_first + [0]
+    for d in order:
+        send(
+            sums.at[pl.ds(up(d) * ys, ys), 1 - c], got_core.at[d],
+            send_1.at[d], recv_1.at[d], sibling,
+        )
+    if ys == 2:
+        for d in range(zs):
+            owner = spot(down(d), 1 - y, c)
+            settled(owner, send_y.at[d], recv_y.at[d])
+            share(owner, sibling, send_c.at[1, d], recv_c.at[1, d])
 
     loads[2].wait()
     loads[3].wait()
@@ -124,39 +204,76 @@
         near_terms(i, x32[i], lambda j: x32[j], diag, near, off, acc)
         return carry
 
-    lax.fori_loop(0, leaves, step, 0, unroll=2)
-    for n in range(rhs):
-        spill = jnp.where(final, 0.0, acc[leaves:, n, :])
-        spill = jnp.concatenate([spill, jnp.zeros((leaves - REACH, width), F32)], axis=0)
-        sums[following, n] = (sums[following, n].astype(F32) + spill).astype(BF16)
+    def joined(d, yy):
+        return sums[up(d) * ys + yy, c].astype(F32) + got_core[d, yy].astype(F32)
+
+    lax.fori_loop(0, 2, step, 0, unroll=2)
+    for d in order:
+        arrived(got_core.at[d], send_1.at[d], recv_1.at[d], sibling)
+        if ys == 2:
+            pass_y[d] = joined(d, 1 - y).astype(BF16)
+            send(pass_y.at[d], got_y.at[d], send_2.at[d], recv_2.at[d], beside)
+    lax.fori_loop(2, 8, step, 0, unroll=2)
+
+    def merged(d):
+        value = joined(d, y)
+        if ys == 2:
+            arrived(got_y.at[d], send_2.at[d], recv_2.at[d], beside)
+            value = value + got_y[d].astype(F32)
+        return value
+
+    for d in far_first:
+        pass_z[d] = merged(d).astype(BF16)
+        send(pass_z.at[d], got_z.at[d], send_3.at[d], recv_3.at[d], column[d - 1])
+    lax.fori_loop(8, leaves - REACH, step, 0, unroll=2)
+
+    for part in range(ys):
+        for d in range(zs):
+            owner = spot(down(d), y if part == 0 else 1 - y, 1 - c)
+            settled(owner, send_c.at[part, d], recv_c.at[part, d])
+    for n in range(rhs):
+        ahead = everything[following, n].astype(F32)[:REACH]
+        x32[leaves:, n, :] = jnp.where(final, 0.0, ahead)
+    lax.fori_loop(leaves - REACH, leaves, step, 0, unroll=2)
+    spill[...] = acc[leaves:]
+    send(spill, got_spill, send_4, recv_4, following)
 
     ids_wide = hits_wide(far_owner[...] * leaves + to_column(far_slot[...]), peers * leaves)
     for n in range(rhs):
         table = everything[:, n].reshape(peers * leaves, width)
         picked[n] = dot(ids_wide, table).astype(BF16)
-    far_pass(picked, v, u, terms)
+    far_pass(picked, v, u, terms, 0, groups)
+
+    arrived(got_spill, send_4, recv_4, preceding)
+    acc[:REACH] += jnp.where(me == 0, 0.0, got_spill[...])
+    total = merged(0)
+    for d in range(1, zs):
+        arrived(got_z.at[d], send_3.at[d], recv_3.at[d], column[d - 1])
+        total = total + got_z[d].astype(F32)
     rows_tall = hits_tall(far_row[...], leaves)
     for n in range(rhs):
-        out[:, n, :] = acc[:leaves, n, :] + scatter_rows(rows_tall, terms[n])
+        out[:, n, :] = acc[:leaves, n, :] + total[n] + scatter_rows(rows_tall, terms[n])
+    for copy in sent:
+        copy.wait_send()
 
 
 def local(panels, diag_blocks, near_blocks, near_offsets, far_u, far_v, far_row, far_owner, far_slot):
     leaves, rhs, width = panels.shape
     pairs = far_row.shape[0]
     peers = lax.axis_size("row")
-    everything = lax.all_gather(jnp.swapaxes(panels, 0, 1), "row", axis=0)
+    ys = 2 if peers == 16 else 1
+    zs = peers // (2 * ys)
     vmem, anywhere = (pl.BlockSpec(memory_space=m) for m in (pltpu.VMEM, pl.ANY))
-    out, sums = pl.pallas_call(
-        kernel,
-        out_shape=(
-            jax.ShapeDtypeStruct(panels.shape, F32),
-            jax.ShapeDtypeStruct((peers, rhs, leaves, width), BF16),
-        ),
+    block = (rhs, leaves, width)
+    sem = pltpu.SemaphoreType.DMA
+    return pl.pallas_call(
+        functools.partial(kernel, (zs, ys)),
+        out_shape=jax.ShapeDtypeStruct(panels.shape, F32),
         in_specs=[
             vmem, anywhere, anywhere, pl.BlockSpec(memory_space=pltpu.SMEM),
-            anywhere, anywhere, vmem, vmem, vmem, vmem,
+            anywhere, anywhere, vmem, vmem, vmem,
         ],
-        out_specs=(vmem, vmem),
+        out_specs=vmem,
         scratch_shapes=[
             pltpu.VMEM(far_u.shape, BF16),
             pltpu.VMEM(far_v.shape, BF16),
@@ -166,15 +283,27 @@
             pltpu.VMEM((leaves + REACH, rhs, width), F32),
             pltpu.VMEM((rhs, pairs, width), BF16),
             pltpu.VMEM((rhs, pairs, width), F32),
-            pltpu.SemaphoreType.DMA((4,)),
+            pltpu.VMEM((peers,) + block, BF16),
+            pltpu.VMEM((peers // 2, 2) + block, BF16),
+            pltpu.VMEM((zs, ys) + block, BF16),
+            pltpu.VMEM((zs,) + block, BF16),
+            pltpu.VMEM((zs,) + block, BF16),
+            pltpu.VMEM((zs,) + block, BF16),
+            pltpu.VMEM((zs,) + block, BF16),
+            pltpu.VMEM((REACH, rhs, width), F32),
+            pltpu.VMEM((REACH, rhs, width), F32),
+            sem((4,)),
+            sem((zs,)), sem((zs,)), sem((zs,)), sem((zs,)), sem((ys, zs)), sem((ys, zs)),
+            sem((zs,)), sem((zs,)), sem((zs,)), sem((zs,)), sem((zs,)), sem((zs,)),
+            sem, sem,
         ],
-        compiler_params=pltpu.CompilerParams(vmem_limit_bytes=56 << 20),
+        compiler_params=pltpu.CompilerParams(
+            vmem_limit_bytes=56 << 20, collective_id=0, has_side_effects=True
+        ),
     )(
         panels, diag_blocks, near_blocks, near_offsets, far_u, far_v,
-        far_row.reshape(1, pairs), far_owner, far_slot.reshape(1, pairs), everything,
+        far_row.reshape(1, pairs), far_owner, far_slot.reshape(1, pairs),
     )
-    got = lax.all_to_all(sums, "row", split_axis=0, concat_axis=0, tiled=True)
-    return out + jnp.swapaxes(jnp.sum(got.astype(F32), axis=0), 0, 1)
 
 
 def solution(mesh):

time: 106 us -> 36.5 us (0.34)
  waiting for transfers between devices: 39.7 us -> 0 us
  blocking collectives: 29.2 us -> 0 us
  Pallas kernels: 16.5 us -> 32 us
  between operations: 13.4 us -> 0.01 us
  local copies, waits for them, and re-layouts: 5.59 us -> 4.36 us
    all_gather x1 -> x0, waiting for transfers between devices: 39 us -> none  [local(): everything = lax.all_gather(jnp.swapaxes(panels, 0, 1), 'row', axis=0)]
    all_to_all x1 -> x0, blocking collectives: 29.2 us -> none  [local(): got = lax.all_to_all(sums, 'row', split_axis=0, concat_axis=0, tiled=True)]
    pallas_call x1, Pallas kernels: 16.5 us -> 32 us  [local(): pl.pallas_call(functools.partial(kernel, (zs, ys)), out_shape=jax.ShapeDt...]
    all_gather x1 -> x0, local copies, waits for them, and re-layouts: 2.78 us -> none  [local(): everything = lax.all_gather(jnp.swapaxes(panels, 0, 1), 'row', axis=0)]
    unnamed x4 -> x3, local copies, waits for them, and re-layouts: 2.81 us -> 4.36 us
  transfers between devices with their start and end apart: 1 -> 0, of which waited for: 1 -> 0; matrix products, arithmetic and copies ran while one was open for 3% -> 0% of each run, Pallas kernels for 0% -> 0%
where the time goes in v2:
time: 36.5 us; the launch traced here: 36.3 us
  Pallas kernels  32 us (88%)
  local copies, waits for them, and re-layouts  4.36 us (12%)
    pallas_call x1, Pallas kernels, local(): pl.pallas_call(functools.partial(kernel, (zs, ys)), out_shape=jax.ShapeDt...  32 us
    unnamed x3, local copies, waits for them, and re-layouts  4.36 us

profile of v2, /device:TPU:0, one launch (start us, length us, event | category | flops | bytes accessed | tf_op | source)
XLA Modules:
  0.0 36.3 jit_solution(4841821693406873277)
XLA Ops:
  0.0 1.3 %copy.10.off = s32[16,2]{1,0:T(8,128)} copy(s32[16,2]{0,1:T(2,128)} %param.12) | data formatting | bytes 256 | tf_op args[3]
  1.3 1.4 %copy.11.far_owner = s32[192,1]{1,0:T(8,128)} copy(s32[192,1]{0,1:T(1,128)} %param.16) | data formatting | bytes 1536 | tf_op args[7]
  2.8 32.0 %shard_map.91 = f32[16,8,256]{2,1,0:T(8,128)} custom-call(bf16[16,8,256]{2,1,0:T(8,128)(2,1)} %panels.1, bf16[16,256,256]{2,1,0:T(8,128)(2,1)} %diag_h.1, bf16[16,2,256,256]{3,2,1,0:T(8,128)(2,1)} %near_h.1, s32[16,2]{1,0:T(8,128)} %copy.10.off, bf16[192,32,256]{2,1,0:T(8,128)(2,1)} %u_h.1, bf16[192,32,256]{2,1,0:T(8,128)(2,1)} %v_h.1, s32[1,192]{1,0:T(1,128)} %bitcast.2, ...), custom_call_target="tpu_custom_call" | custom-call | tf_op jit(solution)/shard_map/pallas_call | solution.py:269
  34.8 1.6 %copy.13 = f32[16,8,256]{2,1,0:T(8,128)} copy(f32[16,8,256]{2,1,0:T(8,128)} %shard_map.91) | data formatting | bytes 262144

commit v3 on v2

--- a/solution.py
+++ b/solution.py
@@ -28,10 +28,6 @@
 
 def to_column(row):
     return jnp.sum(jnp.where(eye(row.shape[1]), row, 0), axis=1, keepdims=True)
-
-
-def to_row(column):
-    return jnp.sum(jnp.where(eye(column.shape[0]), column, 0), axis=0, keepdims=True)
 
 
 def hits_wide(column, count):
@@ -71,22 +67,22 @@
         terms[:, here, :] = dot(inner, two).reshape(rhs, GROUP, width)
         return carry
 
-    lax.fori_loop(begin, end, step, 0, unroll=2)
+    lax.fori_loop(begin, end, step, 0, unroll=6)
 
 
 def near_terms(i, leaf_x, near_x, diag, near, off, acc):
     x = leaf_x.astype(BF16)
     acc[i] += dot(x, diag[i])
     for k in range(near.shape[1]):
-        acc[i] += dot_t(near_x(i + off[i, k]).astype(BF16), near[i, k])
+        acc[i] += dot_t(near_x(i + off[k, i]).astype(BF16), near[i, k])
         back = dot(x, near[i, k])
         for d in range(1, REACH + 1):
-            acc[i + d] += jnp.where(off[i, k] == d, back, 0.0)
+            acc[i + d] += jnp.where(off[k, i] == d, back, 0.0)
 
 
 def kernel(
     shape, panels, diag_h, near_h, off, u_h, v_h, far_row, far_owner, far_slot,
-    out,
+    out, out_far,
     u, v, diag, near, x32, acc, picked, terms, everything, sums,
     got_core, pass_y, got_y, pass_z, got_z, spill, got_spill,
     load_sem, send_z, recv_z, send_y, recv_y, send_c, recv_c,
@@ -97,8 +93,8 @@
         pltpu.make_async_copy(a, b, load_sem.at[s])
         for s, (a, b) in enumerate(((u_h, u), (v_h, v), (near_h, near), (diag_h, diag)))
     ]
-    for load in loads:
-        load.start()
+    loads[0].start()
+    loads[1].start()
     leaves, rhs, width = panels.shape
     peers = everything.shape[0]
     me = lax.axis_index("row")
@@ -164,11 +160,15 @@
         share(me, beside, send_y.at[0], recv_y.at[0])
     share(me, sibling, send_c.at[0, 0], recv_c.at[0, 0])
 
+    ids = far_owner[...] * leaves + far_slot[...]
+    places = hits_tall(ids, peers * leaves)
     rows_wide = hits_wide(to_column(far_row[...]), leaves)
     for n in range(rhs):
         picked[n] = dot(rows_wide, x32[:leaves, n, :].astype(BF16)).astype(BF16)
     loads[0].wait()
     loads[1].wait()
+    loads[2].start()
+    loads[3].start()
     groups = far_row.shape[1] // GROUP
     far_pass(picked, u, v, terms, 0, groups // 2)
     for d in range(1, zs):
@@ -178,8 +178,6 @@
             share(owner, beside, send_y.at[d], recv_y.at[d])
         share(owner, sibling, send_c.at[0, d], recv_c.at[0, d])
     far_pass(picked, u, v, terms, groups // 2, groups)
-    ids = to_row(far_owner[...]) * leaves + far_slot[...]
-    places = hits_tall(ids, peers * leaves)
     for n in range(rhs):
         sums[:, :, n] = scatter_rows(places, terms[n]).astype(BF16).reshape(
             peers // 2, 2, leaves, width
@@ -213,7 +211,7 @@
         if ys == 2:
             pass_y[d] = joined(d, 1 - y).astype(BF16)
             send(pass_y.at[d], got_y.at[d], send_2.at[d], recv_2.at[d], beside)
-    lax.fori_loop(2, 8, step, 0, unroll=2)
+    lax.fori_loop(2, 8, step, 0, unroll=3)
 
     def merged(d):
         value = joined(d, y)
@@ -225,7 +223,7 @@
     for d in far_first:
         pass_z[d] = merged(d).astype(BF16)
         send(pass_z.at[d], got_z.at[d], send_3.at[d], recv_3.at[d], column[d - 1])
-    lax.fori_loop(8, leaves - REACH, step, 0, unroll=2)
+    lax.fori_loop(8, leaves - REACH, step, 0, unroll=4)
 
     for part in range(ys):
         for d in range(zs):
@@ -234,11 +232,11 @@
     for n in range(rhs):
         ahead = everything[following, n].astype(F32)[:REACH]
         x32[leaves:, n, :] = jnp.where(final, 0.0, ahead)
-    lax.fori_loop(leaves - REACH, leaves, step, 0, unroll=2)
+    lax.fori_loop(leaves - REACH, leaves, step, 0, unroll=4)
     spill[...] = acc[leaves:]
     send(spill, got_spill, send_4, recv_4, following)
 
-    ids_wide = hits_wide(far_owner[...] * leaves + to_column(far_slot[...]), peers * leaves)
+    ids_wide = hits_wide(to_column(ids), peers * leaves)
     for n in range(rhs):
         table = everything[:, n].reshape(peers * leaves, width)
         picked[n] = dot(ids_wide, table).astype(BF16)
@@ -252,7 +250,8 @@
         total = total + got_z[d].astype(F32)
     rows_tall = hits_tall(far_row[...], leaves)
     for n in range(rhs):
-        out[:, n, :] = acc[:leaves, n, :] + total[n] + scatter_rows(rows_tall, terms[n])
+        out[:, n, :] = acc[:leaves, n, :] + scatter_rows(rows_tall, terms[n])
+        out_far[:, n, :] = total[n]
     for copy in sent:
         copy.wait_send()
 
@@ -266,14 +265,14 @@
     vmem, anywhere = (pl.BlockSpec(memory_space=m) for m in (pltpu.VMEM, pl.ANY))
     block = (rhs, leaves, width)
     sem = pltpu.SemaphoreType.DMA
-    return pl.pallas_call(
+    near_part, far_part = pl.pallas_call(
         functools.partial(kernel, (zs, ys)),
-        out_shape=jax.ShapeDtypeStruct(panels.shape, F32),
+        out_shape=(jax.ShapeDtypeStruct(panels.shape, F32),) * 2,
         in_specs=[
             vmem, anywhere, anywhere, pl.BlockSpec(memory_space=pltpu.SMEM),
             anywhere, anywhere, vmem, vmem, vmem,
         ],
-        out_specs=vmem,
+        out_specs=(vmem, vmem),
         scratch_shapes=[
             pltpu.VMEM(far_u.shape, BF16),
             pltpu.VMEM(far_v.shape, BF16),
@@ -301,9 +300,10 @@
             vmem_limit_bytes=56 << 20, collective_id=0, has_side_effects=True
         ),
     )(
-        panels, diag_blocks, near_blocks, near_offsets, far_u, far_v,
-        far_row.reshape(1, pairs), far_owner, far_slot.reshape(1, pairs),
+        panels, diag_blocks, near_blocks, near_offsets.T, far_u, far_v,
+        far_row.reshape(1, pairs), far_owner.T, far_slot.reshape(1, pairs),
     )
+    return near_part + far_part
 
 
 def solution(mesh):

time: 36.5 us -> 33 us (0.904)
  local copies, waits for them, and re-layouts: 4.36 us -> 0 us
  other arithmetic: 0 us -> 1.64 us
  Pallas kernels: 32 us -> 31.2 us
    unnamed x3 -> x0, local copies, waits for them, and re-layouts: 4.36 us -> none
    add x0 -> x1, other arithmetic: none -> 1.64 us  [local(): return near_part + far_part]
    pallas_call x1, Pallas kernels: 32 us -> 31.2 us  [local(): pl.pallas_call(functools.partial(kernel, (zs, ys)), out_shape=(jax.ShapeD...]
where the time goes in v3:
time: 33 us; the launch traced here: 32.8 us
  Pallas kernels  31.2 us (95%)
  other arithmetic  1.64 us (5%)
    pallas_call x1, Pallas kernels, local(): pl.pallas_call(functools.partial(kernel, (zs, ys)), out_shape=(jax.ShapeD...  31.2 us
    add x1, other arithmetic, local(): return near_part + far_part  1.64 us

profile of v3, /device:TPU:0, one launch (start us, length us, event | category | flops | bytes accessed | tf_op | source)
XLA Modules:
  0.0 32.8 jit_solution(17022624029390143900)
XLA Ops:
  0.0 31.2 %shard_map.91 = (f32[16,8,256]{2,1,0:T(8,128)}, f32[16,8,256]{2,1,0:T(8,128)}) custom-call(bf16[16,8,256]{2,1,0:T(8,128)(2,1)} %panels.1, bf16[16,256,256]{2,1,0:T(8,128)(2,1)} %diag_h.1, bf16[16,2,256,256]{3,2,1,0:T(8,128)(2,1)} %near_h.1, s32[2,16]{1,0:T(2,128)} %bitcast.4, bf16[192,32,256]{2,1,0:T(8,128)(2,1)} %u_h.1, bf16[192,32,256]{2,1,0:T(8,128)(2,1)} %v_h.1, ...), custom_call_target="tpu_custom_call" | custom-call | tf_op jit(solution)/shard_map/pallas_call | solution.py:268
  31.2 1.6 %add.3 = f32[16,8,256]{2,1,0:T(8,128)} add(f32[16,8,256]{2,1,0:T(8,128)} %get-tuple-element.7, f32[16,8,256]{2,1,0:T(8,128)} %get-tuple-element.8) | non-fusion elementwise | flops 32768 | bytes 393216 | tf_op jit(solution)/shard_map/add | solution.py:306

commit v4 on v3

--- a/solution.py
+++ b/solution.py
@@ -170,30 +170,24 @@
     loads[2].start()
     loads[3].start()
     groups = far_row.shape[1] // GROUP
-    far_pass(picked, u, v, terms, 0, groups // 2)
+    far_pass(picked, u, v, terms, 0, groups)
+    for n in range(rhs):
+        sums[:, :, n] = scatter_rows(places, terms[n]).astype(BF16).reshape(
+            peers // 2, 2, leaves, width
+        )
+
+    order = far_first + [0]
+    for d in order:
+        send(
+            sums.at[pl.ds(up(d) * ys, ys), 1 - c], got_core.at[d],
+            send_1.at[d], recv_1.at[d], sibling,
+        )
     for d in range(1, zs):
         owner = spot(down(d), y, c)
         settled(owner, send_z.at[d], recv_z.at[d])
         if ys == 2:
             share(owner, beside, send_y.at[d], recv_y.at[d])
         share(owner, sibling, send_c.at[0, d], recv_c.at[0, d])
-    far_pass(picked, u, v, terms, groups // 2, groups)
-    for n in range(rhs):
-        sums[:, :, n] = scatter_rows(places, terms[n]).astype(BF16).reshape(
-            peers // 2, 2, leaves, width
-        )
-
-    order = far_first + [0]
-    for d in order:
-        send(
-            sums.at[pl.ds(up(d) * ys, ys), 1 - c], got_core.at[d],
-            send_1.at[d], recv_1.at[d], sibling,
-        )
-    if ys == 2:
-        for d in range(zs):
-            owner = spot(down(d), 1 - y, c)
-            settled(owner, send_y.at[d], recv_y.at[d])
-            share(owner, sibling, send_c.at[1, d], recv_c.at[1, d])
 
     loads[2].wait()
     loads[3].wait()
@@ -212,6 +206,12 @@
             pass_y[d] = joined(d, 1 - y).astype(BF16)
             send(pass_y.at[d], got_y.at[d], send_2.at[d], recv_2.at[d], beside)
     lax.fori_loop(2, 8, step, 0, unroll=3)
+    if ys == 2:
+        for d in range(zs):
+            owner = spot(down(d), 1 - y, c)
+            settled(owner, send_y.at[d], recv_y.at[d])
+            share(owner, sibling, send_c.at[1, d], recv_c.at[1, d])
+
 
     def merged(d):
         value = joined(d, y)

time: 33 us -> 31.1 us (0.942)
  Pallas kernels: 31.2 us -> 29.3 us
    pallas_call x1, Pallas kernels: 31.2 us -> 29.3 us  [local(): pl.pallas_call(functools.partial(kernel, (zs, ys)), out_shape=(jax.ShapeD...]
where the time goes in v4:
time: 31.1 us; the launch traced here: 30.9 us
  Pallas kernels  29.3 us (94%)
  other arithmetic  1.64 us (5%)
    pallas_call x1, Pallas kernels, local(): pl.pallas_call(functools.partial(kernel, (zs, ys)), out_shape=(jax.ShapeD...  29.3 us
    add x1, other arithmetic, local(): return near_part + far_part  1.64 us

profile of v4, /device:TPU:0, one launch (start us, length us, event | category | flops | bytes accessed | tf_op | source)
XLA Modules:
  0.0 30.9 jit_solution(682625520417068756)
XLA Ops:
  0.0 29.3 %shard_map.91 = (f32[16,8,256]{2,1,0:T(8,128)}, f32[16,8,256]{2,1,0:T(8,128)}) custom-call(bf16[16,8,256]{2,1,0:T(8,128)(2,1)} %panels.1, bf16[16,256,256]{2,1,0:T(8,128)(2,1)} %diag_h.1, bf16[16,2,256,256]{3,2,1,0:T(8,128)(2,1)} %near_h.1, s32[2,16]{1,0:T(2,128)} %bitcast.4, bf16[192,32,256]{2,1,0:T(8,128)(2,1)} %u_h.1, bf16[192,32,256]{2,1,0:T(8,128)(2,1)} %v_h.1, ...), custom_call_target="tpu_custom_call" | custom-call | tf_op jit(solution)/shard_map/pallas_call | solution.py:268
  29.3 1.6 %add.3 = f32[16,8,256]{2,1,0:T(8,128)} add(f32[16,8,256]{2,1,0:T(8,128)} %get-tuple-element.7, f32[16,8,256]{2,1,0:T(8,128)} %get-tuple-element.8) | non-fusion elementwise | flops 32768 | bytes 393216 | tf_op jit(solution)/shard_map/add | solution.py:306
